TPU v7x, 32 devices: a whole 2x2x4 slice. The times are simulated.
32 devices in a mesh: store: 4 (over y, x), mod: 8 (over z, core).
Axes of the slice: x: 2, y: 2, z: 4, core: 2. Of those that a mesh axis runs over, the one named last changes fastest.
Arguments:
- act_proj: bfloat16 [256, 256, 512], P(('store', 'mod')), may hold values from -1.5 to 1.5
- grad_proj: bfloat16 [256, 256, 512], P(('store', 'mod')), may hold values from -1.5 to 1.5
- token_mask: int32 [256, 256], P(('store', 'mod')), may hold values 0 or 1
- layer_of: int32 [16], P('mod'), may hold values from 0 to 3, as said below
- layer_weight: float32 [4], replicated, may hold values from 0.25 to 4
- fisher_inv: bfloat16 [16, 1024, 1024], P('mod'), may hold values from -0.2 to 1.8
- stored_grads: bfloat16 [16384, 16384], P('store', 'mod'), may hold values from -0.049804688 to 0.049804688
Outputs:
- scores: float32 [256, 16384], P('mod', 'store')
Inputs may be any that keep to these rules, and one draw needn't show every extreme that they name: `layer_of`: each of the 4 layers holds the same number of modules.
All inputs are finite; a program needn't handle non-finite values. No bound on the sum of `token_mask` on one device may be relied on, other than what follows from the above.
Results may differ from a plain program's by a relative error of at most 0.004.
Values may be sent and summed in bfloat16 or wider, within the bound.
A program may use at most 128 MiB of HBM per device.

v0:
```python
import jax
import jax.numpy as jnp
from jax import lax
from jax.sharding import PartitionSpec as P

R = 32


def local(act_proj, grad_proj, token_mask, layer_of, layer_weight, fisher_inv, stored_grads):
    q_local, length, columns = act_proj.shape
    modules = columns // R
    valid_mask = token_mask.astype(jnp.bfloat16)[:, :, None]
    grad_side = (grad_proj * valid_mask).reshape(q_local, length, modules, R)
    act_side = act_proj.reshape(q_local, length, modules, R)
    per_sample = jnp.einsum(
        "qtmi,qtmj->qmij", grad_side, act_side, preferred_element_type=jnp.float32
    )
    per_sample = per_sample.reshape(q_local, modules, R * R).astype(jnp.bfloat16)
    picked = layer_of[:, None] == jnp.arange(layer_weight.shape[0], dtype=jnp.int32)[None, :]
    module_weight = jnp.sum(jnp.where(picked, layer_weight[None, :], 0.0), axis=1)
    grouped = lax.all_to_all(per_sample, "mod", split_axis=1, concat_axis=0, tiled=True)
    product = jnp.einsum("qkr,krc->qkc", grouped, fisher_inv, preferred_element_type=jnp.float32)
    conditioned = (product * module_weight[None, :, None]).astype(jnp.bfloat16)
    everyone = lax.all_gather(conditioned, "store", axis=0, tiled=True)
    flat_rows = everyone.reshape(everyone.shape[0], -1)
    return lax.psum_scatter(
        lax.dot_general(
            flat_rows, stored_grads, (((1,), (1,)), ((), ())), preferred_element_type=jnp.float32
        ),
        "mod",
        scatter_dimension=0,
        tiled=True,
    )


def solution(mesh):
    in_specs = (
        P(("store", "mod"), None, None),
        P(("store", "mod"), None, None),
        P(("store", "mod"), None),
        P("mod"),
        P(),
        P("mod", None, None),
        P("store", "mod"),
    )
    out_specs = P("mod", "store")
    return jax.shard_map(local, mesh=mesh, in_specs=in_specs, out_specs=out_specs, check_vma=False)
```

profile of v0, /device:TPU:6, one launch (start us, length us, event | category | flops | bytes accessed | tf_op | source)
XLA Modules:
  0.0 130.3 jit_solution(14728193407041983295)
XLA Ops:
  6.5 2.9 %copy.20 = bf16[8,256,512]{1,2,0:T(8,128)(2,1)S(1)} copy(bf16[8,256,512]{2,1,0:T(8,128)(2,1)} %param.8) | data formatting | bytes 4194304 | tf_op args[1]
  9.4 0.0 copy-done.1
  9.4 3.9 %copy.21 = bf16[8,256,512]{1,2,0:T(8,128)(2,1)} copy(bf16[8,256,512]{2,1,0:T(8,128)(2,1)} %param.7) | data formatting | bytes 4194304 | tf_op args[0]
  13.3 0.1 broadcast_multiply_fusion
  13.5 1.4 %copy-done = bf16[8,256,512]{1,2,0:T(8,128)(2,1)S(1)} copy-done((bf16[8,256,512]{1,2,0:T(8,128)(2,1)S(1)}, bf16[8,256,512]{1,2,0:T(8,128)(2,1)}, u32[]{:S(2)}) %copy-start) | copy-done | bytes 2097176
  14.9 0.7 convolution_convert_fusion
  15.6 0.0 copy-start.2
  15.6 0.0 copy-start.3
  15.7 1.1 convert_element_type.17
  16.7 0.9 copy.22
  17.6 4.9 %all-to-all-start = ((bf16[8,16,1024]{2,0,1:T(8,128)(2,1)}), bf16[8,16,1024]{2,0,1:T(8,128)(2,1)S(1)}, u32[]{:S(2)}, u32[]{:S(2)}) async-start(bf16[8,16,1024]{2,0,1:T(8,128)(2,1)} %copy.22), calls=%async_computation | async-start | bytes 524288 | tf_op jit(solution)/shard_map/all_to_all | solution.py:21
  22.5 0.0 all-gather.2.cloned.1.call-start
  22.5 0.0 copy-done.2
  22.5 0.0 copy-done.3
  22.5 0.2 fusion.4
  22.7 9.5 %all-to-all-done = bf16[8,16,1024]{2,0,1:T(8,128)(2,1)S(1)} async-done(((bf16[8,16,1024]{2,0,1:T(8,128)(2,1)}), bf16[8,16,1024]{2,0,1:T(8,128)(2,1)S(1)}, u32[]{:S(2)}, u32[]{:S(2)}) %all-to-all-start) | async-done | bytes 262176 | tf_op jit(solution)/shard_map/all_to_all | solution.py:21
  32.2 3.7 %fusion.1 = bf16[64,2,1024]{2,0,1:T(8,128)(2,1)} fusion(bf16[2,1024,1024]{2,1,0:T(8,128)(2,1)} %param.12, bf16[8,8,2,1024]{3,0,2,1:T(8,128)(2,1)S(1)} %bitcast.20, f32[2]{0:T(128)S(1)} %fusion.4), kind=kOutput, calls=%fused_computation.3 | convolution fusion | flops 268697600 | bytes 4718600 | tf_op jit(solution)/shard_map/qkr,krc->qkc/dot_general | solution.py:22
  36.0 0.0 all-gather.2.cloned.1.call-update
  36.0 0.0 reduce-scatter.2.cloned.1.call-start
  36.0 24.7 %all-gather.2.cloned.1.call-done = bf16[256,2,1024]{2,0,1:T(8,128)(2,1)} async-done(((bf16[64,2,1024]{2,0,1:T(8,128)(2,1)}), bf16[256,2,1024]{2,0,1:T(8,128)(2,1)}) %all-gather.2.cloned.1.call-update) | async-done | bytes 1048592 | tf_op jit(solution)/shard_map/all_gather | solution.py:24
  60.7 1.5 %copy.24 = bf16[256,2,1024]{0,2,1:T(8,128)(2,1)S(1)} copy(bf16[256,2,1024]{2,0,1:T(8,128)(2,1)} %all-gather.2.cloned.1.call-done) | data formatting | bytes 2097152 | tf_op jit(solution)/shard_map/all_gather | solution.py:24
  62.2 10.2 %fusion.5 = f32[256,4096]{1,0:T(8,128)} fusion(bf16[256,2048]{0,1:T(8,128)(2,1)S(1)} %bitcast.21, bf16[4096,2048]{1,0:T(8,128)(2,1)} %param.13), kind=kOutput, calls=%fused_computation.9 | convolution fusion | flops 4294967296 | bytes 22020096 | tf_op jit(solution)/shard_map/dot_general | solution.py:27
  72.3 0.0 reduce-scatter.2.cloned.1.call-update
  72.3 51.1 %reduce-scatter.2.cloned.1.call-done = f32[32,4096]{1,0:T(8,128)} async-done(((f32[256,4096]{1,0:T(8,128)}), f32[32,4096]{1,0:T(8,128)}) %reduce-scatter.2.cloned.1.call-update) | async-done | bytes 524304 | tf_op jit(solution)/shard_map/reduce_scatter | solution.py:26
  (3 shorter events, 0.0 us)
Async XLA Ops:
  6.5 2.9 %copy-start.1 = (s32[8,256]{1,0:T(8,128)S(1)}, s32[8,256]{1,0:T(8,128)}, u32[]{:S(2)}) copy-start(s32[8,256]{1,0:T(8,128)} %param.9) | copy-start | bytes 24580
  13.3 1.6 %copy-start = (bf16[8,256,512]{1,2,0:T(8,128)(2,1)S(1)}, bf16[8,256,512]{1,2,0:T(8,128)(2,1)}, u32[]{:S(2)}) copy-start(bf16[8,256,512]{1,2,0:T(8,128)(2,1)} %copy.21) | copy-start | bytes 6291460
  15.6 6.9 %copy-start.2 = (f32[4]{0:T(128)S(1)}, f32[4]{0:T(128)}, u32[]{:S(2)}) copy-start(f32[4]{0:T(128)} %param.11) | copy-start | bytes 52
  15.6 6.9 %copy-start.3 = (s32[2]{0:T(128)S(1)}, s32[2]{0:T(128)}, u32[]{:S(2)}) copy-start(s32[2]{0:T(128)} %param.10) | copy-start | bytes 28
  17.6 14.6 %all-to-all-start = ((bf16[8,16,1024]{2,0,1:T(8,128)(2,1)}), bf16[8,16,1024]{2,0,1:T(8,128)(2,1)S(1)}, u32[]{:S(2)}, u32[]{:S(2)}) async-start(bf16[8,16,1024]{2,0,1:T(8,128)(2,1)} %copy.22), calls=%async_computation | async-start | bytes 524288 | tf_op jit(solution)/shard_map/all_to_all | solution.py:21
  22.5 38.2 %all-gather.2.cloned.1.call-start = ((), (), s32[]{:S(2)}) async-start(), calls=%async_computation.2 | async-start | bytes 1310720 | tf_op jit(solution)/shard_map/all_gather | solution.py:24
  36.0 87.4 %reduce-scatter.2.cloned.1.call-start = ((), (), s32[]{:S(2)}) async-start(), calls=%async_computation.3 | async-start | bytes 4718592 | tf_op jit(solution)/shard_map/reduce_scatter | solution.py:26
Sparse Core Ops, SparseCore 0:
  36.1 24.5 all-gather.1
  72.5 50.8 reduce-scatter.1
where the time goes:
time: 132 us; the launch traced here: 130 us
  waiting for transfers between devices  85.2 us (65%)
  matrix products  14.6 us (11%)
  between operations  13.5 us (10%)
  local copies, waits for them, and re-layouts  11.7 us (9%)
  starting transfers between devices  4.96 us (4%)
    reduce_scatter x1, waiting for transfers between devices, local(): lax.psum_scatter(lax.dot_general(flat_rows, stored_grads, (((1,), (1,)),...  51.1 us
    all_gather x1, waiting for transfers between devices, local(): everyone = lax.all_gather(conditioned, 'store', axis=0, tiled=True)  24.7 us
    dot_general x1, matrix products, local(): lax.dot_general(flat_rows, stored_grads, (((1,), (1,)), ((), ())), prefer...  10.2 us
    all_to_all x1, waiting for transfers between devices, local(): lax.all_to_all(per_sample, 'mod', split_axis=1, concat_axis=0, tiled=True)  9.5 us
    unnamed x10, local copies, waits for them, and re-layouts  8.25 us
    all_to_all x1, starting transfers between devices, local(): lax.all_to_all(per_sample, 'mod', split_axis=1, concat_axis=0, tiled=True)  4.88 us
    dot_general x1, matrix products, local(): jnp.einsum('qkr,krc->qkc', grouped, fisher_inv, preferred_element_type=jn...  3.74 us
  transfers between devices with their start and end apart: 3, of which 3 were waited for; matrix products, arithmetic and copies ran while one was open for 0% of the time, Pallas kernels for 0%

commit v1 on v0

v1 whole, which is shorter than its diff:
```python
import functools

import jax
import jax.numpy as jnp
from jax import lax
from jax.experimental import pallas as pl
from jax.experimental.pallas import tpu as pltpu
from jax.sharding import PartitionSpec as P

R = 32
MESH = pl.DeviceIdType.MESH


def peer(index, step, count):
    if count & (count - 1):
        return lax.rem(index + step, count)
    other, bit = 0, 1
    while bit < count:
        other = other + ((index // bit + step // bit) % 2) * bit
        bit *= 2
    return other


def kernel(
    n_store, n_mod, width,
    send_ref, layer_ref, weight_ref, fisher_hbm, stored_hbm, out_ref,
    fisher, stored, blocks, everyone, keep, pair_out, pair_in, far_out, far_in,
    fisher_sem, stored_sem, block_send, block_recv, all_send, all_recv,
    pair_send, pair_recv, far_send, far_recv,
):
    s, k = lax.axis_index("store"), lax.axis_index("mod")
    chips = n_mod // 2
    chip, core = k // 2, k % 2
    sibling = k + 1 - 2 * core
    mods, entries = fisher.shape[0], fisher.shape[1]
    owned = out_ref.shape[0]
    samples = stored.shape[0]
    n_chunks = samples // width
    rows = everyone.shape[1]
    q_local = send_ref.shape[1] // mods

    fisher_copy = pltpu.make_async_copy(fisher_hbm, fisher, fisher_sem)
    fisher_copy.start()

    def stored_copy(c):
        part = pl.ds(pl.multiple_of(c * width, width), width)
        return pltpu.make_async_copy(stored_hbm.at[part, :], stored.at[part, :], stored_sem.at[c])

    for c in range(n_chunks):
        stored_copy(c).start()

    barrier = pltpu.get_barrier_semaphore()
    for d in range(1, n_mod):
        pl.semaphore_signal(barrier, inc=1, device_id=(s, peer(k, d, n_mod)), device_id_type=MESH)
    for d in range(1, n_store):
        pl.semaphore_signal(barrier, inc=1, device_id=(peer(s, d, n_store), k), device_id_type=MESH)
    pl.semaphore_wait(barrier, n_mod + n_store - 2)

    block_copies = []
    for d in range(n_mod - 1, 0, -1):
        to = peer(k, d, n_mod)
        copy = pltpu.make_async_remote_copy(
            src_ref=send_ref.at[to], dst_ref=blocks.at[k],
            send_sem=block_send.at[to], recv_sem=block_recv.at[k],
            device_id=(s, to), device_id_type=MESH,
        )
        copy.start()
        block_copies.append(copy)
    blocks[k] = send_ref[k]
    fisher_copy.wait()
    for d in range(1, n_mod):
        source = peer(k, d, n_mod)
        pltpu.make_async_remote_copy(
            src_ref=send_ref.at[source], dst_ref=blocks.at[source],
            send_sem=block_send.at[source], recv_sem=block_recv.at[source],
            device_id=(s, source), device_id_type=MESH,
        ).wait_recv()

    arrived = blocks[...].astype(jnp.float32).reshape(n_mod, mods, q_local, entries)
    for m in range(mods):
        layer = layer_ref[m]
        scale = jnp.float32(0.0)
        for at in range(weight_ref.shape[0]):
            scale = scale + jnp.where(layer == at, weight_ref[at], jnp.float32(0.0))
        mine = arrived[:, m].reshape(n_mod * q_local, entries).astype(jnp.bfloat16)
        product = jnp.dot(mine, fisher[m], preferred_element_type=jnp.float32)
        everyone[s, :, m * entries:(m + 1) * entries] = (product * scale).astype(jnp.bfloat16)

    all_copies = []
    for d in range(1, n_store):
        to = peer(s, d, n_store)
        copy = pltpu.make_async_remote_copy(
            src_ref=everyone.at[s], dst_ref=everyone.at[s],
            send_sem=all_send.at[to], recv_sem=all_recv.at[s],
            device_id=(to, k), device_id_type=MESH,
        )
        copy.start()
        all_copies.append(copy)

    def span(c):
        return pl.ds(pl.multiple_of(c * width, width), width)

    def pair_copy(j, c):
        return pltpu.make_async_remote_copy(
            src_ref=pair_out.at[j, c], dst_ref=pair_in.at[j, c],
            send_sem=pair_send.at[j, c], recv_sem=pair_recv.at[j, c],
            device_id=(s, sibling), device_id_type=MESH,
        )

    def far_copy(j, c):
        return pltpu.make_async_remote_copy(
            src_ref=far_out.at[j, c], dst_ref=far_in.at[chip, c],
            send_sem=far_send.at[j, c], recv_sem=far_recv.at[chip, c],
            device_id=(s, 2 * j + core), device_id_type=MESH,
        )

    def far_arrival(source, c):
        return pltpu.make_async_remote_copy(
            src_ref=far_out.at[source, c], dst_ref=far_in.at[source, c],
            send_sem=far_send.at[source, c], recv_sem=far_recv.at[source, c],
            device_id=(s, 2 * source + core), device_id_type=MESH,
        )

    def finish_pair(step):
        j, c = peer(s, step // n_chunks, n_store), step % n_chunks
        pair_copy(j, c).wait_recv()
        total = keep[j, c] + pair_in[j, c].astype(jnp.float32)

        @pl.when(j == chip)
        def _():
            out_ref[:, span(c)] = total

        @pl.when(j != chip)
        def _():
            far_out[j, c] = total.astype(jnp.bfloat16)
            far_copy(j, c).start()

    def score_step(step, carry):
        t, c = step // n_chunks, step % n_chunks
        j = peer(s, t, n_store)

        @pl.when((c == 0) & (t > 0))
        def _():
            pltpu.make_async_remote_copy(
                src_ref=everyone.at[j], dst_ref=everyone.at[j],
                send_sem=all_send.at[j], recv_sem=all_recv.at[j],
                device_id=(j, k), device_id_type=MESH,
            ).wait_recv()

        @pl.when(t == 0)
        def _():
            stored_copy(c).wait()

        part = lax.dot_general(
            everyone[j], stored[span(c), :], (((1,), (1,)), ((), ())), preferred_element_type=jnp.float32
        )
        low, high = part[:owned], part[owned:]
        first = core == 0
        keep[j, c] = jnp.where(first, low, high)
        pair_out[j, c] = jnp.where(first, high, low).astype(jnp.bfloat16)
        pair_copy(j, c).start()

        @pl.when(step > 0)
        def _():
            finish_pair(step - 1)

        return carry

    steps = n_store * n_chunks
    lax.fori_loop(0, steps, score_step, 0)
    finish_pair(steps - 1)

    for d in range(1, chips):
        source = peer(chip, d, chips)
        for c in range(n_chunks):
            far_arrival(source, c).wait_recv()
            out_ref[:, c * width:(c + 1) * width] += far_in[source, c].astype(jnp.float32)

    for copy in block_copies + all_copies:
        copy.wait_send()
    for j in range(chips):
        for c in range(n_chunks):
            pair_copy(j, c).wait_send()

            @pl.when(j != chip)
            def _():
                far_copy(j, c).wait_send()


def local(n_store, n_mod, act_proj, grad_proj, token_mask, layer_of, layer_weight, fisher_inv, stored_grads):
    q_local, length, columns = act_proj.shape
    modules = columns // R
    mods = modules // n_mod
    valid_mask = token_mask.astype(jnp.bfloat16)[:, :, None]
    grad_side = (grad_proj * valid_mask).reshape(q_local, length, modules, R)
    act_side = act_proj.reshape(q_local, length, modules, R)
    per_sample = jnp.einsum(
        "qtmi,qtmj->qmij", grad_side, act_side, preferred_element_type=jnp.float32
    )
    per_sample = per_sample.reshape(q_local, n_mod, mods, R * R).astype(jnp.bfloat16)
    to_send = per_sample.transpose(1, 2, 0, 3).reshape(n_mod, mods * q_local, R * R)
    samples, depth = stored_grads.shape
    queries = q_local * n_store * n_mod
    owned, rows, chips = queries // n_mod, queries // n_store, n_mod // 2
    assert rows == 2 * owned and chips == n_store
    width = min(1024, samples)
    n_chunks = samples // width
    bf16, f32 = jnp.bfloat16, jnp.float32
    dma = pltpu.SemaphoreType.DMA
    vmem = pl.BlockSpec(memory_space=pltpu.VMEM)
    smem = pl.BlockSpec(memory_space=pltpu.SMEM)
    hbm = pl.BlockSpec(memory_space=pl.ANY)
    return pl.pallas_call(
        functools.partial(kernel, n_store, n_mod, width),
        out_shape=jax.ShapeDtypeStruct((owned, samples), f32),
        in_specs=[vmem, smem, smem, hbm, hbm],
        out_specs=vmem,
        scratch_shapes=[
            pltpu.VMEM(fisher_inv.shape, bf16),
            pltpu.VMEM(stored_grads.shape, bf16),
            pltpu.VMEM(to_send.shape, bf16),
            pltpu.VMEM((n_store, rows, depth), bf16),
            pltpu.VMEM((chips, n_chunks, owned, width), f32),
            pltpu.VMEM((chips, n_chunks, owned, width), bf16),
            pltpu.VMEM((chips, n_chunks, owned, width), bf16),
            pltpu.VMEM((chips, n_chunks, owned, width), bf16),
            pltpu.VMEM((chips, n_chunks, owned, width), bf16),
            dma, dma((n_chunks,)),
            dma((n_mod,)), dma((n_mod,)),
            dma((n_store,)), dma((n_store,)),
            dma((chips, n_chunks)), dma((chips, n_chunks)),
            dma((chips, n_chunks)), dma((chips, n_chunks)),
        ],
        compiler_params=pltpu.CompilerParams(
            collective_id=0, has_side_effects=True, vmem_limit_bytes=56 * 1024 * 1024
        ),
        cost_estimate=pl.CostEstimate(
            flops=2 * queries * samples * depth, bytes_accessed=2 * samples * depth, transcendentals=0
        ),
        name="attribution",
    )(to_send, layer_of, layer_weight, fisher_inv, stored_grads)


def solution(mesh):
    in_specs = (
        P(("store", "mod"), None, None),
        P(("store", "mod"), None, None),
        P(("store", "mod"), None),
        P("mod"),
        P(),
        P("mod", None, None),
        P("store", "mod"),
    )
    out_specs = P("mod", "store")
    body = functools.partial(local, mesh.shape["store"], mesh.shape["mod"])
    return jax.shard_map(body, mesh=mesh, in_specs=in_specs, out_specs=out_specs, check_vma=False)
```

time: 132 us -> 68.5 us (0.52); the launches traced: 130 us -> 68.2 us
  waiting for transfers between devices: 85.2 us -> 0 us
  Pallas kernels: 0 us -> 54.7 us
  matrix products: 14.6 us -> 0.68 us
  between operations: 13.5 us -> 0.05 us
  starting transfers between devices: 4.96 us -> 0 us
    pallas_call x0 -> x1, Pallas kernels: none -> 54.7 us  [local(): pl.pallas_call(functools.partial(kernel, n_store, n_mod, width), out_shap...]
    reduce_scatter x1 -> x0, waiting for transfers between devices: 51.1 us -> none  [local(): lax.psum_scatter(lax.dot_general(flat_rows, stored_grads, (((1,), (1,)),...]
    all_gather x1 -> x0, waiting for transfers between devices: 24.7 us -> none  [local(): everyone = lax.all_gather(conditioned, 'store', axis=0, tiled=True)]
    dot_general x2 -> x0, matrix products: 13.9 us -> none  [the longest x1 10.2 us: local(): lax.dot_general(flat_rows, stored_grads, (((1,), (1,)), ((), ())), prefer...]
    all_to_all x1 -> x0, waiting for transfers between devices: 9.5 us -> none  [local(): lax.all_to_all(per_sample, 'mod', split_axis=1, concat_axis=0, tiled=True)]
    all_to_all x1 -> x0, starting transfers between devices: 4.88 us -> none  [local(): lax.all_to_all(per_sample, 'mod', split_axis=1, concat_axis=0, tiled=True)]
    unnamed x10 -> x5, local copies, waits for them, and re-layouts: 8.25 us -> 10.1 us
    all_gather x1 -> x0, local copies, waits for them, and re-layouts: 1.47 us -> none  [local(): everyone = lax.all_gather(conditioned, 'store', axis=0, tiled=True)]
  transfers between devices with their start and end apart: 3 -> 0, of which waited for: 3 -> 0; matrix products, arithmetic and copies ran while one was open for 0% -> 0% of each run, Pallas kernels for 0% -> 0%
where the time goes in v1:
time: 68.5 us; the launch traced here: 68.2 us
  Pallas kernels  54.7 us (80%)
  local copies, waits for them, and re-layouts  11.9 us (17%)
  other arithmetic  0.84 us (1%)
    pallas_call x1, Pallas kernels, local(): pl.pallas_call(functools.partial(kernel, n_store, n_mod, width), out_shap...  54.7 us
    unnamed x5, local copies, waits for them, and re-layouts  10.1 us
    convert_element_type x2, local copies, waits for them, and re-layouts, local(): per_sample.reshape(q_local, n_mod, mods, R * R).astype(jnp.bfloat16)  1.85 us

profile of v1, /device:TPU:6, one launch (start us, length us, event | category | flops | bytes accessed | tf_op | source)
XLA Modules:
  0.0 68.2 jit_solution(13431183042421327286)
XLA Ops:
  0.0 0.7 %convert_element_type.9 = bf16[8,256]{1,0:T(8,128)(2,1)S(1)} convert(s32[8,256]{1,0:T(8,128)} %param.9) | non-fusion elementwise | flops 2048 | bytes 12288 | tf_op jit(solution)/shard_map/convert_element_type | solution.py:194
  0.7 3.9 %copy.12 = bf16[8,256,512]{1,2,0:T(8,128)(2,1)} copy(bf16[8,256,512]{2,1,0:T(8,128)(2,1)} %param.7) | data formatting | bytes 4194304 | tf_op args[0]
  4.6 2.8 %copy.11 = bf16[8,256,512]{1,2,0:T(8,128)(2,1)S(1)} copy(bf16[8,256,512]{2,1,0:T(8,128)(2,1)} %param.8) | data formatting | bytes 4194304 | tf_op args[1]
  7.5 0.0 copy-start
  7.5 0.1 broadcast_multiply_fusion
  7.6 1.4 %copy-done = bf16[8,256,512]{1,2,0:T(8,128)(2,1)S(1)} copy-done((bf16[8,256,512]{1,2,0:T(8,128)(2,1)S(1)}, bf16[8,256,512]{1,2,0:T(8,128)(2,1)}, u32[]{:S(2)}) %copy-start) | copy-done | bytes 2097176
  9.1 0.7 convolution_convert_fusion
  9.8 1.0 %convert_element_type.11 = bf16[8,8,2,1024]{3,2,1,0:T(2,128)(2,1)S(1)} reshape(bf16[8,16,32,32]{3,2,1,0:T(8,128)(2,1)S(1)} %convolution_convert_fusion) | data formatting | bytes 524288 | tf_op jit(solution)/shard_map/convert_element_type | solution.py:200
  10.8 0.9 %copy.15 = bf16[8,8,2,1024]{3,0,2,1:T(8,128)(2,1)} copy(bf16[8,8,2,1024]{3,2,1,0:T(2,128)(2,1)S(1)} %convert_element_type.11) | data formatting | bytes 524288 | tf_op jit(solution)/shard_map/convert_element_type | solution.py:200
  11.6 54.7 %attribution.1 = f32[32,4096]{1,0:T(8,128)} custom-call(bf16[8,16,1024]{2,1,0:T(8,128)(2,1)} %bitcast.13, s32[2]{0:T(128)} %layer_ref.1, f32[4]{0:T(128)} %weight_ref.1, bf16[2,1024,1024]{2,1,0:T(8,128)(2,1)} %fisher_hbm.1, bf16[4096,2048]{1,0:T(8,128)(2,1)} %stored_hbm.1), custom_call_target="tpu_custom_call" | custom-call | flops 4294967296 | bytes 16777216 | tf_op jit(solution)/shard_map/attribution/pallas_call | solution.py:213
  66.3 1.9 %copy.17 = f32[32,4096]{1,0:T(8,128)} copy(f32[32,4096]{1,0:T(8,128)} %attribution.1) | data formatting | bytes 1048576
Async XLA Ops:
  7.5 1.6 %copy-start = (bf16[8,256,512]{1,2,0:T(8,128)(2,1)S(1)}, bf16[8,256,512]{1,2,0:T(8,128)(2,1)}, u32[]{:S(2)}) copy-start(bf16[8,256,512]{1,2,0:T(8,128)(2,1)} %copy.12) | copy-start | bytes 6291460

commit v2 on v1

--- a/solution.py
+++ b/solution.py
@@ -8,6 +8,7 @@
 from jax.sharding import PartitionSpec as P
 
 R = 32
+LANES = 128
 MESH = pl.DeviceIdType.MESH
 
 
@@ -23,7 +24,8 @@
 
 def kernel(
     n_store, n_mod, width,
-    send_ref, layer_ref, weight_ref, fisher_hbm, stored_hbm, out_ref,
+    act_hbm, grad_hbm, mask_ref, layer_ref, weight_ref, fisher_hbm, stored_hbm, out_ref,
+    act, grad, outer, send_ref, act_sem, grad_sem,
     fisher, stored, blocks, everyone, keep, pair_out, pair_in, far_out, far_in,
     fisher_sem, stored_sem, block_send, block_recv, all_send, all_recv,
     pair_send, pair_recv, far_send, far_recv,
@@ -37,35 +39,90 @@
     samples = stored.shape[0]
     n_chunks = samples // width
     rows = everyone.shape[1]
-    q_local = send_ref.shape[1] // mods
-
-    fisher_copy = pltpu.make_async_copy(fisher_hbm, fisher, fisher_sem)
-    fisher_copy.start()
-
-    def stored_copy(c):
-        part = pl.ds(pl.multiple_of(c * width, width), width)
-        return pltpu.make_async_copy(stored_hbm.at[part, :], stored.at[part, :], stored_sem.at[c])
-
-    for c in range(n_chunks):
-        stored_copy(c).start()
-
+    q_local = mask_ref.shape[0]
+
+    def side_copies(g):
+        lanes = pl.ds(pl.multiple_of(g * LANES, LANES), LANES)
+        return (
+            pltpu.make_async_copy(act_hbm.at[:, :, lanes], act.at[g], act_sem.at[g]),
+            pltpu.make_async_copy(grad_hbm.at[:, :, lanes], grad.at[g], grad_sem.at[g]),
+        )
+
+    def group_at(step):
+        return peer(chip, chips - 1 - step, chips)
+
+    for step in range(chips):
+        for copy in side_copies(group_at(step)):
+            copy.start()
     barrier = pltpu.get_barrier_semaphore()
     for d in range(1, n_mod):
         pl.semaphore_signal(barrier, inc=1, device_id=(s, peer(k, d, n_mod)), device_id_type=MESH)
     for d in range(1, n_store):
         pl.semaphore_signal(barrier, inc=1, device_id=(peer(s, d, n_store), k), device_id_type=MESH)
-    pl.semaphore_wait(barrier, n_mod + n_store - 2)
-
-    block_copies = []
-    for d in range(n_mod - 1, 0, -1):
-        to = peer(k, d, n_mod)
-        copy = pltpu.make_async_remote_copy(
+
+    fisher_copy = pltpu.make_async_copy(fisher_hbm, fisher, fisher_sem)
+
+    def stored_copy(c):
+        part = pl.ds(pl.multiple_of(c * width, width), width)
+        return pltpu.make_async_copy(stored_hbm.at[part, :], stored.at[part, :], stored_sem.at[c])
+
+    def block_copy(to):
+        return pltpu.make_async_remote_copy(
             src_ref=send_ref.at[to], dst_ref=blocks.at[k],
             send_sem=block_send.at[to], recv_sem=block_recv.at[k],
             device_id=(s, to), device_id_type=MESH,
         )
-        copy.start()
-        block_copies.append(copy)
+
+    quarter = lax.broadcasted_iota(jnp.int32, (q_local, LANES), 1) // R
+    per_group = LANES // R
+
+    def outer_step(step, carry):
+        g = group_at(step)
+        for copy in side_copies(g):
+            copy.wait()
+
+        @pl.when(step == 0)
+        def _():
+            fisher_copy.start()
+            for c in range(n_chunks):
+                stored_copy(c).start()
+
+        for q in range(q_local):
+            valid = mask_ref[q:q + 1, :].astype(jnp.float32)
+            turned = (grad[g, q].astype(jnp.float32).T * valid).astype(jnp.bfloat16)
+            outer[q * LANES:(q + 1) * LANES, :] = jnp.dot(
+                turned, act[g, q], preferred_element_type=jnp.float32
+            )
+
+        def flat(a, part):
+            row = None
+            for r in range(per_group):
+                line = outer[pl.ds(a * R + part * per_group + r, q_local, stride=LANES), :]
+                shift = (R * (r - a)) % LANES
+                if shift:
+                    line = pltpu.roll(line, shift, 1)
+                row = line if row is None else jnp.where(quarter == r, line, row)
+            return row
+
+        for half in range(2):
+            for part in range(entries // LANES):
+                lines = [flat(half * mods + m, part) for m in range(mods)]
+                send_ref[2 * g + half, :, part * LANES:(part + 1) * LANES] = jnp.concatenate(
+                    lines, axis=0
+                ).astype(jnp.bfloat16)
+
+        @pl.when(step == 0)
+        def _():
+            pl.semaphore_wait(barrier, n_mod + n_store - 2)
+
+        for half in range(2):
+            @pl.when(2 * g + half != k)
+            def _():
+                block_copy(2 * g + half).start()
+
+        return carry
+
+    lax.fori_loop(0, chips, outer_step, 0)
     blocks[k] = send_ref[k]
     fisher_copy.wait()
     for d in range(1, n_mod):
@@ -124,7 +181,7 @@
     def finish_pair(step):
         j, c = peer(s, step // n_chunks, n_store), step % n_chunks
         pair_copy(j, c).wait_recv()
-        total = keep[j, c] + pair_in[j, c].astype(jnp.float32)
+        total = keep[step % 2] + pair_in[j, c].astype(jnp.float32)
 
         @pl.when(j == chip)
         def _():
@@ -156,7 +213,7 @@
         )
         low, high = part[:owned], part[owned:]
         first = core == 0
-        keep[j, c] = jnp.where(first, low, high)
+        keep[step % 2] = jnp.where(first, low, high)
         pair_out[j, c] = jnp.where(first, high, low).astype(jnp.bfloat16)
         pair_copy(j, c).start()
 
@@ -176,7 +233,9 @@
             far_arrival(source, c).wait_recv()
             out_ref[:, c * width:(c + 1) * width] += far_in[source, c].astype(jnp.float32)
 
-    for copy in block_copies + all_copies:
+    for d in range(1, n_mod):
+        block_copy(peer(k, d, n_mod)).wait_send()
+    for copy in all_copies:
         copy.wait_send()
     for j in range(chips):
         for c in range(n_chunks):
@@ -189,20 +248,11 @@
 
 def local(n_store, n_mod, act_proj, grad_proj, token_mask, layer_of, layer_weight, fisher_inv, stored_grads):
     q_local, length, columns = act_proj.shape
-    modules = columns // R
-    mods = modules // n_mod
-    valid_mask = token_mask.astype(jnp.bfloat16)[:, :, None]
-    grad_side = (grad_proj * valid_mask).reshape(q_local, length, modules, R)
-    act_side = act_proj.reshape(q_local, length, modules, R)
-    per_sample = jnp.einsum(
-        "qtmi,qtmj->qmij", grad_side, act_side, preferred_element_type=jnp.float32
-    )
-    per_sample = per_sample.reshape(q_local, n_mod, mods, R * R).astype(jnp.bfloat16)
-    to_send = per_sample.transpose(1, 2, 0, 3).reshape(n_mod, mods * q_local, R * R)
+    mods, entries = fisher_inv.shape[0], fisher_inv.shape[1]
     samples, depth = stored_grads.shape
     queries = q_local * n_store * n_mod
     owned, rows, chips = queries // n_mod, queries // n_store, n_mod // 2
-    assert rows == 2 * owned and chips == n_store
+    assert rows == 2 * owned and chips == n_store and columns == chips * LANES and 2 * mods * R == LANES
     width = min(1024, samples)
     n_chunks = samples // width
     bf16, f32 = jnp.bfloat16, jnp.float32
@@ -213,14 +263,19 @@
     return pl.pallas_call(
         functools.partial(kernel, n_store, n_mod, width),
         out_shape=jax.ShapeDtypeStruct((owned, samples), f32),
-        in_specs=[vmem, smem, smem, hbm, hbm],
+        in_specs=[hbm, hbm, vmem, smem, smem, hbm, hbm],
         out_specs=vmem,
         scratch_shapes=[
+            pltpu.VMEM((chips, q_local, length, LANES), bf16),
+            pltpu.VMEM((chips, q_local, length, LANES), bf16),
+            pltpu.VMEM((q_local * LANES, LANES), f32),
+            pltpu.VMEM((n_mod, mods * q_local, entries), bf16),
+            dma((chips,)), dma((chips,)),
             pltpu.VMEM(fisher_inv.shape, bf16),
             pltpu.VMEM(stored_grads.shape, bf16),
-            pltpu.VMEM(to_send.shape, bf16),
+            pltpu.VMEM((n_mod, mods * q_local, entries), bf16),
             pltpu.VMEM((n_store, rows, depth), bf16),
-            pltpu.VMEM((chips, n_chunks, owned, width), f32),
+            pltpu.VMEM((2, owned, width), f32),
             pltpu.VMEM((chips, n_chunks, owned, width), bf16),
             pltpu.VMEM((chips, n_chunks, owned, width), bf16),
             pltpu.VMEM((chips, n_chunks, owned, width), bf16),
@@ -238,7 +293,7 @@
             flops=2 * queries * samples * depth, bytes_accessed=2 * samples * depth, transcendentals=0
         ),
         name="attribution",
-    )(to_send, layer_of, layer_weight, fisher_inv, stored_grads)
+    )(act_proj, grad_proj, token_mask, layer_of, layer_weight, fisher_inv, stored_grads)
 
 
 def solution(mesh):

time: 68.5 us -> 56.1 us (0.82)
  local copies, waits for them, and re-layouts: 11.9 us -> 1.87 us
  other arithmetic: 0.84 us -> 0 us
  Pallas kernels: 54.7 us -> 54 us
    unnamed x5 -> x1, local copies, waits for them, and re-layouts: 10.1 us -> 1.87 us
    convert_element_type x2 -> x0, local copies, waits for them, and re-layouts: 1.85 us -> none  [local(): per_sample.reshape(q_local, n_mod, mods, R * R).astype(jnp.bfloat16)]
    convert_element_type x1 -> x0, other arithmetic: 0.7 us -> none  [local(): valid_mask = token_mask.astype(jnp.bfloat16)[:, :, None]]
where the time goes in v2:
time: 56.1 us; the launch traced here: 55.9 us
  Pallas kernels  54 us (96%)
  local copies, waits for them, and re-layouts  1.87 us (3%)
    pallas_call x1, Pallas kernels, local(): pl.pallas_call(functools.partial(kernel, n_store, n_mod, width), out_shap...  54 us
    unnamed x1, local copies, waits for them, and re-layouts  1.87 us

profile of v2, /device:TPU:6, one launch (start us, length us, event | category | flops | bytes accessed | tf_op | source)
XLA Modules:
  0.0 55.9 jit_solution(3681752763581490551)
XLA Ops:
  0.0 54.0 %attribution.1 = f32[32,4096]{1,0:T(8,128)} custom-call(bf16[8,256,512]{2,1,0:T(8,128)(2,1)} %act_hbm.1, bf16[8,256,512]{2,1,0:T(8,128)(2,1)} %grad_hbm.1, s32[8,256]{1,0:T(8,128)} %mask_ref.1, s32[2]{0:T(128)} %layer_ref.1, f32[4]{0:T(128)} %weight_ref.1, bf16[2,1024,1024]{2,1,0:T(8,128)(2,1)} %fisher_hbm.1, bf16[4096,2048]{1,0:T(8,128)(2,1)} %stored_hbm.1), custom_call_target="tpu_custom_call" | custom-call | flops 4294967296 | bytes 16777216 | tf_op jit(solution)/shard_map/attribution/pallas_call | solution.py:263
  54.0 1.9 %copy.9 = f32[32,4096]{1,0:T(8,128)} copy(f32[32,4096]{1,0:T(8,128)} %attribution.1) | data formatting | bytes 1048576

commit v3 on v2

--- a/solution.py
+++ b/solution.py
@@ -9,6 +9,7 @@
 
 R = 32
 LANES = 128
+HOP = 2
 MESH = pl.DeviceIdType.MESH
 
 
@@ -20,6 +21,13 @@
         other = other + ((index // bit + step // bit) % 2) * bit
         bit *= 2
     return other
+
+
+def turn(step, count):
+    if count & (count - 1) or count < 4:
+        return step
+    half = count // 2
+    return (step % 2) * half + step // 2
 
 
 def kernel(
@@ -133,6 +141,14 @@
             device_id=(s, source), device_id_type=MESH,
         ).wait_recv()
 
+    def gather_copy(to, origin, m):
+        part = everyone.at[origin, :, m * entries:(m + 1) * entries]
+        return pltpu.make_async_remote_copy(
+            src_ref=part, dst_ref=part,
+            send_sem=all_send.at[to, m], recv_sem=all_recv.at[origin, m],
+            device_id=(to, k), device_id_type=MESH,
+        )
+
     arrived = blocks[...].astype(jnp.float32).reshape(n_mod, mods, q_local, entries)
     for m in range(mods):
         layer = layer_ref[m]
@@ -142,17 +158,8 @@
         mine = arrived[:, m].reshape(n_mod * q_local, entries).astype(jnp.bfloat16)
         product = jnp.dot(mine, fisher[m], preferred_element_type=jnp.float32)
         everyone[s, :, m * entries:(m + 1) * entries] = (product * scale).astype(jnp.bfloat16)
-
-    all_copies = []
-    for d in range(1, n_store):
-        to = peer(s, d, n_store)
-        copy = pltpu.make_async_remote_copy(
-            src_ref=everyone.at[s], dst_ref=everyone.at[s],
-            send_sem=all_send.at[to], recv_sem=all_recv.at[s],
-            device_id=(to, k), device_id_type=MESH,
-        )
-        copy.start()
-        all_copies.append(copy)
+        for d in range(1, n_store):
+            gather_copy(peer(s, turn(d, n_store), n_store), s, m).start()
 
     def span(c):
         return pl.ds(pl.multiple_of(c * width, width), width)
@@ -165,44 +172,57 @@
         )
 
     def far_copy(j, c):
+        up = j > chip
+        to = jnp.where(up, chip + 1, chip - 1)
+        slot = jnp.where(up | (to != j), j, chips)
         return pltpu.make_async_remote_copy(
-            src_ref=far_out.at[j, c], dst_ref=far_in.at[chip, c],
-            send_sem=far_send.at[j, c], recv_sem=far_recv.at[chip, c],
-            device_id=(s, 2 * j + core), device_id_type=MESH,
-        )
-
-    def far_arrival(source, c):
-        return pltpu.make_async_remote_copy(
-            src_ref=far_out.at[source, c], dst_ref=far_in.at[source, c],
-            send_sem=far_send.at[source, c], recv_sem=far_recv.at[source, c],
-            device_id=(s, 2 * source + core), device_id_type=MESH,
-        )
-
-    def finish_pair(step):
-        j, c = peer(s, step // n_chunks, n_store), step % n_chunks
+            src_ref=far_out.at[j, c], dst_ref=far_in.at[slot, c],
+            send_sem=far_send.at[j, c], recv_sem=far_recv.at[slot, c],
+            device_id=(s, 2 * to + core), device_id_type=MESH,
+        )
+
+    def add_arrival(slot, c, kept):
+        pltpu.make_async_remote_copy(
+            src_ref=far_out.at[0, c], dst_ref=far_in.at[slot, c],
+            send_sem=far_send.at[0, c], recv_sem=far_recv.at[slot, c],
+            device_id=(s, sibling), device_id_type=MESH,
+        ).wait_recv()
+        keep[kept] += far_in[slot, c].astype(jnp.float32)
+
+    def where_is(step):
+        return peer(s, turn(step // n_chunks, n_store), n_store), step % n_chunks
+
+    def finish(step):
+        j, c = where_is(step)
+        kept = step % keep.shape[0]
         pair_copy(j, c).wait_recv()
-        total = keep[step % 2] + pair_in[j, c].astype(jnp.float32)
+        keep[kept] += pair_in[j, c].astype(jnp.float32)
+
+        @pl.when(((j >= chip) & (chip > 0)) | ((j < chip) & (chip < chips - 1)))
+        def _():
+            add_arrival(j, c, kept)
+
+        @pl.when((j == chip) & (chip < chips - 1))
+        def _():
+            add_arrival(chips, c, kept)
 
         @pl.when(j == chip)
         def _():
-            out_ref[:, span(c)] = total
+            out_ref[:, span(c)] = keep[kept]
 
         @pl.when(j != chip)
         def _():
-            far_out[j, c] = total.astype(jnp.bfloat16)
+            far_out[j, c] = keep[kept].astype(jnp.bfloat16)
             far_copy(j, c).start()
 
-    def score_step(step, carry):
-        t, c = step // n_chunks, step % n_chunks
-        j = peer(s, t, n_store)
+    def score(step):
+        t = step // n_chunks
+        j, c = where_is(step)
 
         @pl.when((c == 0) & (t > 0))
         def _():
-            pltpu.make_async_remote_copy(
-                src_ref=everyone.at[j], dst_ref=everyone.at[j],
-                send_sem=all_send.at[j], recv_sem=all_recv.at[j],
-                device_id=(j, k), device_id_type=MESH,
-            ).wait_recv()
+            for m in range(mods):
+                gather_copy(j, j, m).wait_recv()
 
         @pl.when(t == 0)
         def _():
@@ -213,30 +233,41 @@
         )
         low, high = part[:owned], part[owned:]
         first = core == 0
-        keep[step % 2] = jnp.where(first, low, high)
+        keep[step % keep.shape[0]] = jnp.where(first, low, high)
         pair_out[j, c] = jnp.where(first, high, low).astype(jnp.bfloat16)
         pair_copy(j, c).start()
 
-        @pl.when(step > 0)
-        def _():
-            finish_pair(step - 1)
-
+    steps = n_store * n_chunks
+    gap = n_chunks
+
+    def turn_of_loop(i, carry):
+        @pl.when((i < n_chunks) | ((i >= n_chunks + gap) & (i < steps + gap)))
+        def _():
+            score(jnp.where(i < n_chunks, i, i - gap))
+
+        def finish_at(hops, inner):
+            at = i - 1 - hops * HOP
+            step = jnp.where(at < n_chunks, at, at - gap)
+            j, _ = where_is(jnp.maximum(step, 0))
+            depth = jnp.where(j > chip, chip, chips - 1 - chip)
+            depth = jnp.where(j == chip, jnp.maximum(chip, chips - 1 - chip), depth)
+
+            @pl.when((((at >= 0) & (at < n_chunks)) | ((at >= n_chunks + gap) & (at < steps + gap))) & (depth == hops))
+            def _():
+                finish(step)
+
+            return inner
+
+        lax.fori_loop(0, chips, finish_at, 0)
         return carry
 
-    steps = n_store * n_chunks
-    lax.fori_loop(0, steps, score_step, 0)
-    finish_pair(steps - 1)
-
-    for d in range(1, chips):
-        source = peer(chip, d, chips)
-        for c in range(n_chunks):
-            far_arrival(source, c).wait_recv()
-            out_ref[:, c * width:(c + 1) * width] += far_in[source, c].astype(jnp.float32)
+    lax.fori_loop(0, steps + gap + 1 + (chips - 1) * HOP, turn_of_loop, 0)
 
     for d in range(1, n_mod):
         block_copy(peer(k, d, n_mod)).wait_send()
-    for copy in all_copies:
-        copy.wait_send()
+    for d in range(1, n_store):
+        for m in range(mods):
+            gather_copy(peer(s, d, n_store), s, m).wait_send()
     for j in range(chips):
         for c in range(n_chunks):
             pair_copy(j, c).wait_send()
@@ -275,19 +306,19 @@
             pltpu.VMEM(stored_grads.shape, bf16),
             pltpu.VMEM((n_mod, mods * q_local, entries), bf16),
             pltpu.VMEM((n_store, rows, depth), bf16),
-            pltpu.VMEM((2, owned, width), f32),
+            pltpu.VMEM((2 + (chips - 1) * HOP, owned, width), f32),
             pltpu.VMEM((chips, n_chunks, owned, width), bf16),
             pltpu.VMEM((chips, n_chunks, owned, width), bf16),
             pltpu.VMEM((chips, n_chunks, owned, width), bf16),
-            pltpu.VMEM((chips, n_chunks, owned, width), bf16),
+            pltpu.VMEM((chips + 1, n_chunks, owned, width), bf16),
             dma, dma((n_chunks,)),
             dma((n_mod,)), dma((n_mod,)),
-            dma((n_store,)), dma((n_store,)),
+            dma((n_store, mods)), dma((n_store, mods)),
             dma((chips, n_chunks)), dma((chips, n_chunks)),
-            dma((chips, n_chunks)), dma((chips, n_chunks)),
+            dma((chips, n_chunks)), dma((chips + 1, n_chunks)),
         ],
         compiler_params=pltpu.CompilerParams(
-            collective_id=0, has_side_effects=True, vmem_limit_bytes=56 * 1024 * 1024
+            collective_id=0, has_side_effects=True, vmem_limit_bytes=60 * 1024 * 1024
         ),
         cost_estimate=pl.CostEstimate(
             flops=2 * queries * samples * depth, bytes_accessed=2 * samples * depth, transcendentals=0

time: 56.1 us -> 62.3 us (1.11)
  Pallas kernels: 54 us -> 60.2 us
    pallas_call x1, Pallas kernels: 54 us -> 60.2 us  [local(): pl.pallas_call(functools.partial(kernel, n_store, n_mod, width), out_shap...]
where the time goes in v3:
time: 62.3 us; the launch traced here: 62.1 us
  Pallas kernels  60.2 us (97%)
  local copies, waits for them, and re-layouts  1.87 us (3%)
    pallas_call x1, Pallas kernels, local(): pl.pallas_call(functools.partial(kernel, n_store, n_mod, width), out_shap...  60.2 us
    unnamed x1, local copies, waits for them, and re-layouts  1.87 us

profile of v3, /device:TPU:6, one launch (start us, length us, event | category | flops | bytes accessed | tf_op | source)
XLA Modules:
  0.0 62.1 jit_solution(16374701820132493959)
XLA Ops:
  0.0 60.2 %attribution.1 = f32[32,4096]{1,0:T(8,128)} custom-call(bf16[8,256,512]{2,1,0:T(8,128)(2,1)} %act_hbm.1, bf16[8,256,512]{2,1,0:T(8,128)(2,1)} %grad_hbm.1, s32[8,256]{1,0:T(8,128)} %mask_ref.1, s32[2]{0:T(128)} %layer_ref.1, f32[4]{0:T(128)} %weight_ref.1, bf16[2,1024,1024]{2,1,0:T(8,128)(2,1)} %fisher_hbm.1, bf16[4096,2048]{1,0:T(8,128)(2,1)} %stored_hbm.1), custom_call_target="tpu_custom_call" | custom-call | flops 4294967296 | bytes 16777216 | tf_op jit(solution)/shard_map/attribution/pallas_call | solution.py:294
  60.3 1.9 %copy.9 = f32[32,4096]{1,0:T(8,128)} copy(f32[32,4096]{1,0:T(8,128)} %attribution.1) | data formatting | bytes 1048576

commit v4 on v3

--- a/solution.py
+++ b/solution.py
@@ -9,7 +9,6 @@
 
 R = 32
 LANES = 128
-HOP = 2
 MESH = pl.DeviceIdType.MESH
 
 
@@ -23,18 +22,11 @@
     return other
 
 
-def turn(step, count):
-    if count & (count - 1) or count < 4:
-        return step
-    half = count // 2
-    return (step % 2) * half + step // 2
-
-
 def kernel(
-    n_store, n_mod, width,
+    n_store, n_mod, deep,
     act_hbm, grad_hbm, mask_ref, layer_ref, weight_ref, fisher_hbm, stored_hbm, out_ref,
     act, grad, outer, send_ref, act_sem, grad_sem,
-    fisher, stored, blocks, everyone, keep, pair_out, pair_in, far_out, far_in,
+    fisher, stored, blocks, everyone, raw, keep, pair_out, pair_in, far_out, far_in,
     fisher_sem, stored_sem, block_send, block_recv, all_send, all_recv,
     pair_send, pair_recv, far_send, far_recv,
 ):
@@ -45,6 +37,8 @@
     mods, entries = fisher.shape[0], fisher.shape[1]
     owned = out_ref.shape[0]
     samples = stored.shape[0]
+    per = LANES // owned
+    width = per * deep
     n_chunks = samples // width
     rows = everyone.shape[1]
     q_local = mask_ref.shape[0]
@@ -62,6 +56,7 @@
     for step in range(chips):
         for copy in side_copies(group_at(step)):
             copy.start()
+    raw[...] = jnp.zeros_like(raw)
     barrier = pltpu.get_barrier_semaphore()
     for d in range(1, n_mod):
         pl.semaphore_signal(barrier, inc=1, device_id=(s, peer(k, d, n_mod)), device_id_type=MESH)
@@ -141,12 +136,12 @@
             device_id=(s, source), device_id_type=MESH,
         ).wait_recv()
 
-    def gather_copy(to, origin, m):
-        part = everyone.at[origin, :, m * entries:(m + 1) * entries]
+    def gather_copy(t, m):
+        lanes = pl.ds(m * entries, entries)
         return pltpu.make_async_remote_copy(
-            src_ref=part, dst_ref=part,
-            send_sem=all_send.at[to, m], recv_sem=all_recv.at[origin, m],
-            device_id=(to, k), device_id_type=MESH,
+            src_ref=everyone.at[0, :, lanes], dst_ref=everyone.at[t, :, lanes],
+            send_sem=all_send.at[t, m], recv_sem=all_recv.at[t, m],
+            device_id=(peer(s, t, n_store), k), device_id_type=MESH,
         )
 
     arrived = blocks[...].astype(jnp.float32).reshape(n_mod, mods, q_local, entries)
@@ -157,9 +152,9 @@
             scale = scale + jnp.where(layer == at, weight_ref[at], jnp.float32(0.0))
         mine = arrived[:, m].reshape(n_mod * q_local, entries).astype(jnp.bfloat16)
         product = jnp.dot(mine, fisher[m], preferred_element_type=jnp.float32)
-        everyone[s, :, m * entries:(m + 1) * entries] = (product * scale).astype(jnp.bfloat16)
-        for d in range(1, n_store):
-            gather_copy(peer(s, turn(d, n_store), n_store), s, m).start()
+        everyone[0, :, m * entries:(m + 1) * entries] = (product * scale).astype(jnp.bfloat16)
+        for d in range(n_store - 1, 0, -1):
+            gather_copy(d, m).start()
 
     def span(c):
         return pl.ds(pl.multiple_of(c * width, width), width)
@@ -181,93 +176,118 @@
             device_id=(s, 2 * to + core), device_id_type=MESH,
         )
 
-    def add_arrival(slot, c, kept):
+    def add_arrival(j, slot, c):
         pltpu.make_async_remote_copy(
             src_ref=far_out.at[0, c], dst_ref=far_in.at[slot, c],
             send_sem=far_send.at[0, c], recv_sem=far_recv.at[slot, c],
             device_id=(s, sibling), device_id_type=MESH,
         ).wait_recv()
-        keep[kept] += far_in[slot, c].astype(jnp.float32)
-
-    def where_is(step):
-        return peer(s, turn(step // n_chunks, n_store), n_store), step % n_chunks
-
-    def finish(step):
-        j, c = where_is(step)
-        kept = step % keep.shape[0]
+        keep[j, c] += far_in[slot, c].astype(jnp.float32)
+
+    def finish(j, c):
         pair_copy(j, c).wait_recv()
-        keep[kept] += pair_in[j, c].astype(jnp.float32)
+        keep[j, c] += pair_in[j, c].astype(jnp.float32)
 
         @pl.when(((j >= chip) & (chip > 0)) | ((j < chip) & (chip < chips - 1)))
         def _():
-            add_arrival(j, c, kept)
+            add_arrival(j, j, c)
 
         @pl.when((j == chip) & (chip < chips - 1))
         def _():
-            add_arrival(chips, c, kept)
+            add_arrival(j, chips, c)
 
         @pl.when(j == chip)
         def _():
-            out_ref[:, span(c)] = keep[kept]
+            turned = keep[j, c].T
+            for a in range(per):
+                lanes = pl.ds(pl.multiple_of(c * width + a * deep, LANES), deep)
+                out_ref[:, lanes] = turned[a * owned:(a + 1) * owned]
 
         @pl.when(j != chip)
         def _():
-            far_out[j, c] = keep[kept].astype(jnp.bfloat16)
+            far_out[j, c] = keep[j, c].astype(jnp.bfloat16)
             far_copy(j, c).start()
 
-    def score(step):
-        t = step // n_chunks
-        j, c = where_is(step)
-
-        @pl.when((c == 0) & (t > 0))
-        def _():
-            for m in range(mods):
-                gather_copy(j, j, m).wait_recv()
-
-        @pl.when(t == 0)
-        def _():
-            stored_copy(c).wait()
-
-        part = lax.dot_general(
-            everyone[j], stored[span(c), :], (((1,), (1,)), ((), ())), preferred_element_type=jnp.float32
-        )
-        low, high = part[:owned], part[owned:]
+    part_of_lane = lax.broadcasted_iota(jnp.int32, (deep, LANES), 1) // owned
+
+    def side_by_side(at):
+        column, offset = at // LANES * LANES, at % LANES
+        block = None
+        for a in range(per):
+            piece = raw[a * deep:(a + 1) * deep, column:column + LANES]
+            shift = (a * owned - offset) % LANES
+            if shift:
+                piece = pltpu.roll(piece, shift, 1)
+            block = piece if block is None else jnp.where(part_of_lane == a, piece, block)
+        return block
+
+    def pair_off(j, c, at):
+        low, high = side_by_side(at), side_by_side(at + owned)
         first = core == 0
-        keep[step % keep.shape[0]] = jnp.where(first, low, high)
+        keep[j, c] = jnp.where(first, low, high)
         pair_out[j, c] = jnp.where(first, high, low).astype(jnp.bfloat16)
         pair_copy(j, c).start()
 
-    steps = n_store * n_chunks
-    gap = n_chunks
+    def scores(queries, c):
+        raw[:, :queries.shape[0]] = lax.dot_general(
+            stored[span(c), :], queries, (((1,), (1,)), ((), ())), preferred_element_type=jnp.float32
+        )
+
+    order = list(range(n_store - 1, 0, -1))
+    second = n_chunks + chips - 1
 
     def turn_of_loop(i, carry):
-        @pl.when((i < n_chunks) | ((i >= n_chunks + gap) & (i < steps + gap)))
-        def _():
-            score(jnp.where(i < n_chunks, i, i - gap))
+        @pl.when(i < n_chunks)
+        def _():
+            stored_copy(i).wait()
+            scores(everyone[0], i)
+            pair_off(s, i, 0)
+
+        @pl.when(i == second)
+        def _():
+            for t in order:
+                for m in range(mods):
+                    gather_copy(t, m).wait_recv()
+
+        @pl.when((i >= second) & (i < second + n_chunks))
+        def _():
+            c = i - second
+            scores(everyone[1:].reshape((n_store - 1) * rows, -1), c)
+            for t in order:
+                pair_off(peer(s, t, n_store), c, (t - 1) * rows)
 
         def finish_at(hops, inner):
-            at = i - 1 - hops * HOP
-            step = jnp.where(at < n_chunks, at, at - gap)
-            j, _ = where_is(jnp.maximum(step, 0))
-            depth = jnp.where(j > chip, chip, chips - 1 - chip)
-            depth = jnp.where(j == chip, jnp.maximum(chip, chips - 1 - chip), depth)
-
-            @pl.when((((at >= 0) & (at < n_chunks)) | ((at >= n_chunks + gap) & (at < steps + gap))) & (depth == hops))
+            at = i - 1 - hops
+
+            def item(j, c):
+                depth = jnp.where(j > chip, chip, chips - 1 - chip)
+                depth = jnp.where(j == chip, jnp.maximum(chip, chips - 1 - chip), depth)
+
+                @pl.when(depth == hops)
+                def _():
+                    finish(j, c)
+
+            @pl.when((at >= 0) & (at < n_chunks))
             def _():
-                finish(step)
+                item(s, at)
+
+            @pl.when((at >= second) & (at < second + n_chunks))
+            def _():
+                for t in order:
+                    item(peer(s, t, n_store), at - second)
 
             return inner
 
         lax.fori_loop(0, chips, finish_at, 0)
         return carry
 
-    lax.fori_loop(0, steps + gap + 1 + (chips - 1) * HOP, turn_of_loop, 0)
+    lax.fori_loop(0, second + n_chunks + chips, turn_of_loop, 0)
 
     for d in range(1, n_mod):
         block_copy(peer(k, d, n_mod)).wait_send()
     for d in range(1, n_store):
         for m in range(mods):
-            gather_copy(peer(s, d, n_store), s, m).wait_send()
+            gather_copy(d, m).wait_send()
     for j in range(chips):
         for c in range(n_chunks):
             pair_copy(j, c).wait_send()
@@ -284,15 +304,17 @@
     queries = q_local * n_store * n_mod
     owned, rows, chips = queries // n_mod, queries // n_store, n_mod // 2
     assert rows == 2 * owned and chips == n_store and columns == chips * LANES and 2 * mods * R == LANES
-    width = min(1024, samples)
-    n_chunks = samples // width
+    assert n_store & (n_store - 1) == 0 and n_mod & (n_mod - 1) == 0 and LANES % owned == 0
+    deep = 256
+    n_chunks = samples // (deep * (LANES // owned))
+    wide = -(-(n_store - 1) * rows // LANES) * LANES
     bf16, f32 = jnp.bfloat16, jnp.float32
     dma = pltpu.SemaphoreType.DMA
     vmem = pl.BlockSpec(memory_space=pltpu.VMEM)
     smem = pl.BlockSpec(memory_space=pltpu.SMEM)
     hbm = pl.BlockSpec(memory_space=pl.ANY)
     return pl.pallas_call(
-        functools.partial(kernel, n_store, n_mod, width),
+        functools.partial(kernel, n_store, n_mod, deep),
         out_shape=jax.ShapeDtypeStruct((owned, samples), f32),
         in_specs=[hbm, hbm, vmem, smem, smem, hbm, hbm],
         out_specs=vmem,
@@ -306,11 +328,12 @@
             pltpu.VMEM(stored_grads.shape, bf16),
             pltpu.VMEM((n_mod, mods * q_local, entries), bf16),
             pltpu.VMEM((n_store, rows, depth), bf16),
-            pltpu.VMEM((2 + (chips - 1) * HOP, owned, width), f32),
-            pltpu.VMEM((chips, n_chunks, owned, width), bf16),
-            pltpu.VMEM((chips, n_chunks, owned, width), bf16),
-            pltpu.VMEM((chips, n_chunks, owned, width), bf16),
-            pltpu.VMEM((chips + 1, n_chunks, owned, width), bf16),
+            pltpu.VMEM((deep * (LANES // owned), wide), f32),
+            pltpu.VMEM((chips, n_chunks, deep, LANES), f32),
+            pltpu.VMEM((chips, n_chunks, deep, LANES), bf16),
+            pltpu.VMEM((chips, n_chunks, deep, LANES), bf16),
+            pltpu.VMEM((chips, n_chunks, deep, LANES), bf16),
+            pltpu.VMEM((chips + 1, n_chunks, deep, LANES), bf16),
             dma, dma((n_chunks,)),
             dma((n_mod,)), dma((n_mod,)),
             dma((n_store, mods)), dma((n_store, mods)),
@@ -318,7 +341,7 @@
             dma((chips, n_chunks)), dma((chips + 1, n_chunks)),
         ],
         compiler_params=pltpu.CompilerParams(
-            collective_id=0, has_side_effects=True, vmem_limit_bytes=60 * 1024 * 1024
+            collective_id=0, has_side_effects=True, vmem_limit_bytes=(56 if chips <= 4 else 63) * 1024 * 1024
         ),
         cost_estimate=pl.CostEstimate(
             flops=2 * queries * samples * depth, bytes_accessed=2 * samples * depth, transcendentals=0

time: 62.3 us -> 60.6 us (0.973)
  Pallas kernels: 60.2 us -> 58.5 us
    pallas_call x1, Pallas kernels: 60.2 us -> 58.5 us  [local(): pl.pallas_call(functools.partial(kernel, n_store, n_mod, deep), out_shape...]
where the time goes in v4:
time: 60.6 us; the launch traced here: 60.4 us
  Pallas kernels  58.5 us (97%)
  local copies, waits for them, and re-layouts  1.87 us (3%)
    pallas_call x1, Pallas kernels, local(): pl.pallas_call(functools.partial(kernel, n_store, n_mod, deep), out_shape...  58.5 us
    unnamed x1, local copies, waits for them, and re-layouts  1.87 us

profile of v4, /device:TPU:6, one launch (start us, length us, event | category | flops | bytes accessed | tf_op | source)
XLA Modules:
  0.0 60.4 jit_solution(3063491589433414830)
XLA Ops:
  0.0 58.5 %attribution.1 = f32[32,4096]{1,0:T(8,128)} custom-call(bf16[8,256,512]{2,1,0:T(8,128)(2,1)} %act_hbm.1, bf16[8,256,512]{2,1,0:T(8,128)(2,1)} %grad_hbm.1, s32[8,256]{1,0:T(8,128)} %mask_ref.1, s32[2]{0:T(128)} %layer_ref.1, f32[4]{0:T(128)} %weight_ref.1, bf16[2,1024,1024]{2,1,0:T(8,128)(2,1)} %fisher_hbm.1, bf16[4096,2048]{1,0:T(8,128)(2,1)} %stored_hbm.1), custom_call_target="tpu_custom_call" | custom-call | flops 4294967296 | bytes 16777216 | tf_op jit(solution)/shard_map/attribution/pallas_call | solution.py:316
  58.5 1.9 %copy.9 = f32[32,4096]{1,0:T(8,128)} copy(f32[32,4096]{1,0:T(8,128)} %attribution.1) | data formatting | bytes 1048576

commit v5 on v4

--- a/solution.py
+++ b/solution.py
@@ -9,6 +9,8 @@
 
 R = 32
 LANES = 128
+PARTS = 2
+GAP = 2
 MESH = pl.DeviceIdType.MESH
 
 
@@ -37,10 +39,11 @@
     mods, entries = fisher.shape[0], fisher.shape[1]
     owned = out_ref.shape[0]
     samples = stored.shape[0]
+    owned = owned // PARTS
     per = LANES // owned
     width = per * deep
     n_chunks = samples // width
-    rows = everyone.shape[1]
+    rows = everyone.shape[2]
     q_local = mask_ref.shape[0]
 
     def side_copies(g):
@@ -128,33 +131,35 @@
     lax.fori_loop(0, chips, outer_step, 0)
     blocks[k] = send_ref[k]
     fisher_copy.wait()
-    for d in range(1, n_mod):
-        source = peer(k, d, n_mod)
-        pltpu.make_async_remote_copy(
-            src_ref=send_ref.at[source], dst_ref=blocks.at[source],
-            send_sem=block_send.at[source], recv_sem=block_recv.at[source],
-            device_id=(s, source), device_id_type=MESH,
-        ).wait_recv()
-
-    def gather_copy(t, m):
+    def gather_copy(u, t, m):
         lanes = pl.ds(m * entries, entries)
         return pltpu.make_async_remote_copy(
-            src_ref=everyone.at[0, :, lanes], dst_ref=everyone.at[t, :, lanes],
-            send_sem=all_send.at[t, m], recv_sem=all_recv.at[t, m],
+            src_ref=everyone.at[u, 0, :, lanes], dst_ref=everyone.at[u, t, :, lanes],
+            send_sem=all_send.at[u, t, m], recv_sem=all_recv.at[u, t, m],
             device_id=(peer(s, t, n_store), k), device_id_type=MESH,
         )
 
-    arrived = blocks[...].astype(jnp.float32).reshape(n_mod, mods, q_local, entries)
-    for m in range(mods):
-        layer = layer_ref[m]
-        scale = jnp.float32(0.0)
-        for at in range(weight_ref.shape[0]):
-            scale = scale + jnp.where(layer == at, weight_ref[at], jnp.float32(0.0))
-        mine = arrived[:, m].reshape(n_mod * q_local, entries).astype(jnp.bfloat16)
-        product = jnp.dot(mine, fisher[m], preferred_element_type=jnp.float32)
-        everyone[0, :, m * entries:(m + 1) * entries] = (product * scale).astype(jnp.bfloat16)
-        for d in range(n_store - 1, 0, -1):
-            gather_copy(d, m).start()
+    for u in range(PARTS):
+        sources = [h * chips + u * (chips // PARTS) + b for h in range(2) for b in range(chips // PARTS)]
+        for source in sources:
+            @pl.when(k != source)
+            def _():
+                pltpu.make_async_remote_copy(
+                    src_ref=send_ref.at[source], dst_ref=blocks.at[source],
+                    send_sem=block_send.at[source], recv_sem=block_recv.at[source],
+                    device_id=(s, source), device_id_type=MESH,
+                ).wait_recv()
+        arrived = [blocks[source].astype(jnp.float32) for source in sources]
+        for m in range(mods):
+            layer = layer_ref[m]
+            scale = jnp.float32(0.0)
+            for at in range(weight_ref.shape[0]):
+                scale = scale + jnp.where(layer == at, weight_ref[at], jnp.float32(0.0))
+            mine = jnp.concatenate([one[m * q_local:(m + 1) * q_local] for one in arrived], axis=0)
+            product = jnp.dot(mine.astype(jnp.bfloat16), fisher[m], preferred_element_type=jnp.float32)
+            everyone[u, 0, :, m * entries:(m + 1) * entries] = (product * scale).astype(jnp.bfloat16)
+            for t in range(n_store - 1, 0, -1):
+                gather_copy(u, t, m).start()
 
     def span(c):
         return pl.ds(pl.multiple_of(c * width, width), width)
@@ -199,9 +204,10 @@
         @pl.when(j == chip)
         def _():
             turned = keep[j, c].T
+            part = pl.ds(pl.multiple_of(c // n_chunks * owned, owned), owned)
             for a in range(per):
-                lanes = pl.ds(pl.multiple_of(c * width + a * deep, LANES), deep)
-                out_ref[:, lanes] = turned[a * owned:(a + 1) * owned]
+                lanes = pl.ds(pl.multiple_of(c % n_chunks * width + a * deep, LANES), deep)
+                out_ref[part, lanes] = turned[a * owned:(a + 1) * owned]
 
         @pl.when(j != chip)
         def _():
@@ -228,68 +234,62 @@
         pair_out[j, c] = jnp.where(first, high, low).astype(jnp.bfloat16)
         pair_copy(j, c).start()
 
-    def scores(queries, c):
-        raw[:, :queries.shape[0]] = lax.dot_general(
-            stored[span(c), :], queries, (((1,), (1,)), ((), ())), preferred_element_type=jnp.float32
-        )
-
-    order = list(range(n_store - 1, 0, -1))
-    second = n_chunks + chips - 1
+    order = list(range(n_store - 1, -1, -1))
+    steps = PARTS * n_chunks
+    every = n_chunks + GAP
 
     def turn_of_loop(i, carry):
-        @pl.when(i < n_chunks)
-        def _():
-            stored_copy(i).wait()
-            scores(everyone[0], i)
-            pair_off(s, i, 0)
-
-        @pl.when(i == second)
-        def _():
+        u, c = i // every, i % every
+
+        @pl.when((c == 0) & (u < PARTS))
+        def _():
+            for t in range(1, n_store):
+                for m in range(mods):
+                    gather_copy(u, t, m).wait_recv()
+
+        @pl.when((c < n_chunks) & (u == 0))
+        def _():
+            stored_copy(c).wait()
+
+        @pl.when((c < n_chunks) & (u < PARTS))
+        def _():
+            queries = everyone[u].reshape(n_store * rows, -1)
+            raw[:, :n_store * rows] = lax.dot_general(
+                stored[span(c), :], queries, (((1,), (1,)), ((), ())), preferred_element_type=jnp.float32
+            )
             for t in order:
-                for m in range(mods):
-                    gather_copy(t, m).wait_recv()
-
-        @pl.when((i >= second) & (i < second + n_chunks))
-        def _():
-            c = i - second
-            scores(everyone[1:].reshape((n_store - 1) * rows, -1), c)
-            for t in order:
-                pair_off(peer(s, t, n_store), c, (t - 1) * rows)
+                pair_off(peer(s, t, n_store), u * n_chunks + c, t * rows)
 
         def finish_at(hops, inner):
             at = i - 1 - hops
-
-            def item(j, c):
-                depth = jnp.where(j > chip, chip, chips - 1 - chip)
-                depth = jnp.where(j == chip, jnp.maximum(chip, chips - 1 - chip), depth)
-
-                @pl.when(depth == hops)
-                def _():
-                    finish(j, c)
-
-            @pl.when((at >= 0) & (at < n_chunks))
-            def _():
-                item(s, at)
-
-            @pl.when((at >= second) & (at < second + n_chunks))
+            v, c = at // every, at % every
+
+            @pl.when((at >= 0) & (v < PARTS) & (c < n_chunks))
             def _():
                 for t in order:
-                    item(peer(s, t, n_store), at - second)
+                    j = peer(s, t, n_store)
+                    depth = jnp.where(j > chip, chip, chips - 1 - chip)
+                    depth = jnp.where(j == chip, jnp.maximum(chip, chips - 1 - chip), depth)
+
+                    @pl.when(depth == hops)
+                    def _():
+                        finish(j, v * n_chunks + c)
 
             return inner
 
         lax.fori_loop(0, chips, finish_at, 0)
         return carry
 
-    lax.fori_loop(0, second + n_chunks + chips, turn_of_loop, 0)
+    lax.fori_loop(0, PARTS * every + chips, turn_of_loop, 0)
 
     for d in range(1, n_mod):
         block_copy(peer(k, d, n_mod)).wait_send()
     for d in range(1, n_store):
-        for m in range(mods):
-            gather_copy(d, m).wait_send()
+        for u in range(PARTS):
+            for m in range(mods):
+                gather_copy(u, d, m).wait_send()
     for j in range(chips):
-        for c in range(n_chunks):
+        for c in range(steps):
             pair_copy(j, c).wait_send()
 
             @pl.when(j != chip)
@@ -305,9 +305,11 @@
     owned, rows, chips = queries // n_mod, queries // n_store, n_mod // 2
     assert rows == 2 * owned and chips == n_store and columns == chips * LANES and 2 * mods * R == LANES
     assert n_store & (n_store - 1) == 0 and n_mod & (n_mod - 1) == 0 and LANES % owned == 0
-    deep = 256
-    n_chunks = samples // (deep * (LANES // owned))
-    wide = -(-(n_store - 1) * rows // LANES) * LANES
+    deep = 128
+    per = LANES // (owned // PARTS)
+    n_chunks = samples // (deep * per)
+    steps = PARTS * n_chunks
+    wide = -(-queries // PARTS // LANES) * LANES
     bf16, f32 = jnp.bfloat16, jnp.float32
     dma = pltpu.SemaphoreType.DMA
     vmem = pl.BlockSpec(memory_space=pltpu.VMEM)
@@ -327,18 +329,18 @@
             pltpu.VMEM(fisher_inv.shape, bf16),
             pltpu.VMEM(stored_grads.shape, bf16),
             pltpu.VMEM((n_mod, mods * q_local, entries), bf16),
-            pltpu.VMEM((n_store, rows, depth), bf16),
-            pltpu.VMEM((deep * (LANES // owned), wide), f32),
-            pltpu.VMEM((chips, n_chunks, deep, LANES), f32),
-            pltpu.VMEM((chips, n_chunks, deep, LANES), bf16),
-            pltpu.VMEM((chips, n_chunks, deep, LANES), bf16),
-            pltpu.VMEM((chips, n_chunks, deep, LANES), bf16),
-            pltpu.VMEM((chips + 1, n_chunks, deep, LANES), bf16),
+            pltpu.VMEM((PARTS, n_store, rows // PARTS, depth), bf16),
+            pltpu.VMEM((deep * per, wide), f32),
+            pltpu.VMEM((chips, steps, deep, LANES), f32),
+            pltpu.VMEM((chips, steps, deep, LANES), bf16),
+            pltpu.VMEM((chips, steps, deep, LANES), bf16),
+            pltpu.VMEM((chips, steps, deep, LANES), bf16),
+            pltpu.VMEM((chips + 1, steps, deep, LANES), bf16),
             dma, dma((n_chunks,)),
             dma((n_mod,)), dma((n_mod,)),
-            dma((n_store, mods)), dma((n_store, mods)),
-            dma((chips, n_chunks)), dma((chips, n_chunks)),
-            dma((chips, n_chunks)), dma((chips + 1, n_chunks)),
+            dma((PARTS, n_store, mods)), dma((PARTS, n_store, mods)),
+            dma((chips, steps)), dma((chips, steps)),
+            dma((chips, steps)), dma((chips + 1, steps)),
         ],
         compiler_params=pltpu.CompilerParams(
             collective_id=0, has_side_effects=True, vmem_limit_bytes=(56 if chips <= 4 else 63) * 1024 * 1024

time: 60.6 us -> 65.4 us (1.079)
  the two profiles are of different devices: /device:TPU:6 before, /device:TPU:0 now
where the time goes in v5:
time: 65.4 us; the launch traced here: 65.2 us
  Pallas kernels  63.3 us (97%)
  local copies, waits for them, and re-layouts  1.87 us (3%)
    pallas_call x1, Pallas kernels, local(): pl.pallas_call(functools.partial(kernel, n_store, n_mod, deep), out_shape...  63.3 us
    unnamed x1, local copies, waits for them, and re-layouts  1.87 us

profile of v5, /device:TPU:0, one launch (start us, length us, event | category | flops | bytes accessed | tf_op | source)
XLA Modules:
  0.0 65.2 jit_solution(10484055466564837822)
XLA Ops:
  0.0 63.3 %attribution.1 = f32[32,4096]{1,0:T(8,128)} custom-call(bf16[8,256,512]{2,1,0:T(8,128)(2,1)} %act_hbm.1, bf16[8,256,512]{2,1,0:T(8,128)(2,1)} %grad_hbm.1, s32[8,256]{1,0:T(8,128)} %mask_ref.1, s32[2]{0:T(128)} %layer_ref.1, f32[4]{0:T(128)} %weight_ref.1, bf16[2,1024,1024]{2,1,0:T(8,128)(2,1)} %fisher_hbm.1, bf16[4096,2048]{1,0:T(8,128)(2,1)} %stored_hbm.1), custom_call_target="tpu_custom_call" | custom-call | flops 4294967296 | bytes 16777216 | tf_op jit(solution)/shard_map/attribution/pallas_call | solution.py:318
  63.3 1.9 %copy.9 = f32[32,4096]{1,0:T(8,128)} copy(f32[32,4096]{1,0:T(8,128)} %attribution.1) | data formatting | bytes 1048576

commit v6 on v4

--- a/solution.py
+++ b/solution.py
@@ -153,7 +153,7 @@
         mine = arrived[:, m].reshape(n_mod * q_local, entries).astype(jnp.bfloat16)
         product = jnp.dot(mine, fisher[m], preferred_element_type=jnp.float32)
         everyone[0, :, m * entries:(m + 1) * entries] = (product * scale).astype(jnp.bfloat16)
-        for d in range(n_store - 1, 0, -1):
+        for d in range(1, n_store):
             gather_copy(d, m).start()
 
     def span(c):
@@ -167,45 +167,22 @@
         )
 
     def far_copy(j, c):
-        up = j > chip
-        to = jnp.where(up, chip + 1, chip - 1)
-        slot = jnp.where(up | (to != j), j, chips)
         return pltpu.make_async_remote_copy(
-            src_ref=far_out.at[j, c], dst_ref=far_in.at[slot, c],
-            send_sem=far_send.at[j, c], recv_sem=far_recv.at[slot, c],
-            device_id=(s, 2 * to + core), device_id_type=MESH,
-        )
-
-    def add_arrival(j, slot, c):
-        pltpu.make_async_remote_copy(
-            src_ref=far_out.at[0, c], dst_ref=far_in.at[slot, c],
-            send_sem=far_send.at[0, c], recv_sem=far_recv.at[slot, c],
-            device_id=(s, sibling), device_id_type=MESH,
-        ).wait_recv()
-        keep[j, c] += far_in[slot, c].astype(jnp.float32)
+            src_ref=far_out.at[j, c], dst_ref=far_in.at[chip, c],
+            send_sem=far_send.at[j, c], recv_sem=far_recv.at[chip, c],
+            device_id=(s, 2 * j + core), device_id_type=MESH,
+        )
 
     def finish(j, c):
         pair_copy(j, c).wait_recv()
-        keep[j, c] += pair_in[j, c].astype(jnp.float32)
-
-        @pl.when(((j >= chip) & (chip > 0)) | ((j < chip) & (chip < chips - 1)))
-        def _():
-            add_arrival(j, j, c)
-
-        @pl.when((j == chip) & (chip < chips - 1))
-        def _():
-            add_arrival(j, chips, c)
 
         @pl.when(j == chip)
         def _():
-            turned = keep[j, c].T
-            for a in range(per):
-                lanes = pl.ds(pl.multiple_of(c * width + a * deep, LANES), deep)
-                out_ref[:, lanes] = turned[a * owned:(a + 1) * owned]
+            keep[j, c] += pair_in[j, c].astype(jnp.float32)
 
         @pl.when(j != chip)
         def _():
-            far_out[j, c] = keep[j, c].astype(jnp.bfloat16)
+            far_out[j, c] = (keep[j, c] + pair_in[j, c].astype(jnp.float32)).astype(jnp.bfloat16)
             far_copy(j, c).start()
 
     part_of_lane = lax.broadcasted_iota(jnp.int32, (deep, LANES), 1) // owned
@@ -233,55 +210,50 @@
             stored[span(c), :], queries, (((1,), (1,)), ((), ())), preferred_element_type=jnp.float32
         )
 
-    order = list(range(n_store - 1, 0, -1))
-    second = n_chunks + chips - 1
-
-    def turn_of_loop(i, carry):
-        @pl.when(i < n_chunks)
-        def _():
-            stored_copy(i).wait()
-            scores(everyone[0], i)
-            pair_off(s, i, 0)
-
-        @pl.when(i == second)
-        def _():
-            for t in order:
+    bounds = [0, 1, min(3, n_store), n_store]
+    for first_t, end_t in zip(bounds[:-1], bounds[1:]):
+        if first_t == end_t:
+            continue
+        if first_t:
+            for t in range(first_t, end_t):
                 for m in range(mods):
                     gather_copy(t, m).wait_recv()
 
-        @pl.when((i >= second) & (i < second + n_chunks))
-        def _():
-            c = i - second
-            scores(everyone[1:].reshape((n_store - 1) * rows, -1), c)
-            for t in order:
-                pair_off(peer(s, t, n_store), c, (t - 1) * rows)
-
-        def finish_at(hops, inner):
-            at = i - 1 - hops
-
-            def item(j, c):
-                depth = jnp.where(j > chip, chip, chips - 1 - chip)
-                depth = jnp.where(j == chip, jnp.maximum(chip, chips - 1 - chip), depth)
-
-                @pl.when(depth == hops)
-                def _():
-                    finish(j, c)
-
-            @pl.when((at >= 0) & (at < n_chunks))
+        def step(c, carry, first_t=first_t, end_t=end_t):
+            if first_t == 0:
+                stored_copy(c).wait()
+            scores(everyone[first_t:end_t].reshape((end_t - first_t) * rows, -1), c)
+            for t in range(end_t - 1, first_t - 1, -1):
+                pair_off(peer(s, t, n_store), c, (t - first_t) * rows)
+
+            @pl.when(c > 0)
             def _():
-                item(s, at)
-
-            @pl.when((at >= second) & (at < second + n_chunks))
-            def _():
-                for t in order:
-                    item(peer(s, t, n_store), at - second)
-
-            return inner
-
-        lax.fori_loop(0, chips, finish_at, 0)
+                for t in range(end_t - 1, first_t - 1, -1):
+                    finish(peer(s, t, n_store), c - 1)
+
+            return carry
+
+        lax.fori_loop(0, n_chunks, step, 0)
+        for t in range(end_t - 1, first_t - 1, -1):
+            finish(peer(s, t, n_store), n_chunks - 1)
+
+    def own_sum(c, carry):
+        total = keep[chip, c]
+        for d in range(1, chips):
+            source = peer(chip, d, chips)
+            pltpu.make_async_remote_copy(
+                src_ref=far_out.at[source, c], dst_ref=far_in.at[source, c],
+                send_sem=far_send.at[source, c], recv_sem=far_recv.at[source, c],
+                device_id=(s, 2 * source + core), device_id_type=MESH,
+            ).wait_recv()
+            total = total + far_in[source, c].astype(jnp.float32)
+        turned = total.T
+        for a in range(per):
+            lanes = pl.ds(pl.multiple_of(c * width + a * deep, LANES), deep)
+            out_ref[:, lanes] = turned[a * owned:(a + 1) * owned]
         return carry
 
-    lax.fori_loop(0, second + n_chunks + chips, turn_of_loop, 0)
+    lax.fori_loop(0, n_chunks, own_sum, 0)
 
     for d in range(1, n_mod):
         block_copy(peer(k, d, n_mod)).wait_send()
@@ -333,12 +305,12 @@
             pltpu.VMEM((chips, n_chunks, deep, LANES), bf16),
             pltpu.VMEM((chips, n_chunks, deep, LANES), bf16),
             pltpu.VMEM((chips, n_chunks, deep, LANES), bf16),
-            pltpu.VMEM((chips + 1, n_chunks, deep, LANES), bf16),
+            pltpu.VMEM((chips, n_chunks, deep, LANES), bf16),
             dma, dma((n_chunks,)),
             dma((n_mod,)), dma((n_mod,)),
             dma((n_store, mods)), dma((n_store, mods)),
             dma((chips, n_chunks)), dma((chips, n_chunks)),
-            dma((chips, n_chunks)), dma((chips + 1, n_chunks)),
+            dma((chips, n_chunks)), dma((chips, n_chunks)),
         ],
         compiler_params=pltpu.CompilerParams(
             collective_id=0, has_side_effects=True, vmem_limit_bytes=(56 if chips <= 4 else 63) * 1024 * 1024

time: 60.6 us -> 55.1 us (0.909)
  Pallas kernels: 58.5 us -> 52.8 us
    pallas_call x1, Pallas kernels: 58.5 us -> 52.8 us  [local(): pl.pallas_call(functools.partial(kernel, n_store, n_mod, deep), out_shape...]
where the time goes in v6:
time: 55.1 us; the launch traced here: 54.6 us
  Pallas kernels  52.8 us (96%)
  local copies, waits for them, and re-layouts  1.87 us (3%)
    pallas_call x1, Pallas kernels, local(): pl.pallas_call(functools.partial(kernel, n_store, n_mod, deep), out_shape...  52.8 us
    unnamed x1, local copies, waits for them, and re-layouts  1.87 us

profile of v6, /device:TPU:6, one launch (start us, length us, event | category | flops | bytes accessed | tf_op | source)
XLA Modules:
  0.0 54.6 jit_solution(3786999271517633096)
XLA Ops:
  0.0 52.8 %attribution.1 = f32[32,4096]{1,0:T(8,128)} custom-call(bf16[8,256,512]{2,1,0:T(8,128)(2,1)} %act_hbm.1, bf16[8,256,512]{2,1,0:T(8,128)(2,1)} %grad_hbm.1, s32[8,256]{1,0:T(8,128)} %mask_ref.1, s32[2]{0:T(128)} %layer_ref.1, f32[4]{0:T(128)} %weight_ref.1, bf16[2,1024,1024]{2,1,0:T(8,128)(2,1)} %fisher_hbm.1, bf16[4096,2048]{1,0:T(8,128)(2,1)} %stored_hbm.1), custom_call_target="tpu_custom_call" | custom-call | flops 4294967296 | bytes 16777216 | tf_op jit(solution)/shard_map/attribution/pallas_call | solution.py:288
  52.8 1.9 %copy.9 = f32[32,4096]{1,0:T(8,128)} copy(f32[32,4096]{1,0:T(8,128)} %attribution.1) | data formatting | bytes 1048576

commit v7 on v6

--- a/solution.py
+++ b/solution.py
@@ -91,8 +91,8 @@
                 stored_copy(c).start()
 
         for q in range(q_local):
-            valid = mask_ref[q:q + 1, :].astype(jnp.float32)
-            turned = (grad[g, q].astype(jnp.float32).T * valid).astype(jnp.bfloat16)
+            valid = mask_ref[q:q + 1, :].astype(jnp.bfloat16)
+            turned = grad[g, q].T * valid
             outer[q * LANES:(q + 1) * LANES, :] = jnp.dot(
                 turned, act[g, q], preferred_element_type=jnp.float32
             )

time: 55.1 us -> 55.1 us (level)
  no operation moved by 1% of the time
where the time goes in v7:
time: 55.1 us; the launch traced here: 54.6 us
  Pallas kernels  52.8 us (96%)
  local copies, waits for them, and re-layouts  1.87 us (3%)
    pallas_call x1, Pallas kernels, local(): pl.pallas_call(functools.partial(kernel, n_store, n_mod, deep), out_shape...  52.8 us
    unnamed x1, local copies, waits for them, and re-layouts  1.87 us

profile of v7, /device:TPU:6, one launch (start us, length us, event | category | flops | bytes accessed | tf_op | source)
XLA Modules:
  0.0 54.6 jit_solution(5461203391614207960)
XLA Ops:
  0.0 52.8 %attribution.1 = f32[32,4096]{1,0:T(8,128)} custom-call(bf16[8,256,512]{2,1,0:T(8,128)(2,1)} %act_hbm.1, bf16[8,256,512]{2,1,0:T(8,128)(2,1)} %grad_hbm.1, s32[8,256]{1,0:T(8,128)} %mask_ref.1, s32[2]{0:T(128)} %layer_ref.1, f32[4]{0:T(128)} %weight_ref.1, bf16[2,1024,1024]{2,1,0:T(8,128)(2,1)} %fisher_hbm.1, bf16[4096,2048]{1,0:T(8,128)(2,1)} %stored_hbm.1), custom_call_target="tpu_custom_call" | custom-call | flops 4294967296 | bytes 16777216 | tf_op jit(solution)/shard_map/attribution/pallas_call | solution.py:288
  52.8 1.9 %copy.9 = f32[32,4096]{1,0:T(8,128)} copy(f32[32,4096]{1,0:T(8,128)} %attribution.1) | data formatting | bytes 1048576
